TPU v7x, 32 devices: a whole 2x2x4 slice. The times are simulated.
32 devices in a mesh: groups: 2 (over x), region: 16 (over z, y, core).
Axes of the slice: x: 2, y: 2, z: 4, core: 2. Of those that a mesh axis runs over, the one named last changes fastest.
Arguments:
- environment: bfloat16 [160, 96, 3264], P(('groups', 'region')), parts along dimension 0, may hold values from -6 to 6
- site_tensors: bfloat16 [160, 1, 4, 96, 96], P(('groups', 'region')), parts along dimension 0, may hold values from -0.625 to 0.625
- operator_blocks: bfloat16 [34, 4, 34], replicated, may hold values from -0.5 to 0.5
- join_in: int32 [80, 4], P('groups'), parts along dimension 0, may hold values from -1 to 39, as said below
- block_sizes: int32 [80], P('groups'), parts along dimension 0, may hold values from 48 to 96
Outputs:
- advanced: bfloat16 [160, 96, 3264], P(('groups', 'region')), parts along dimension 0
There are 2 independent parts, one for each index of `groups`. A program takes and returns all parts, laid end to end along the dimension named above; an argument that names none is the same for every part. Nothing has to cross between parts.
Inputs may be any that keep to these rules, and one draw needn't show every extreme that they name: Sectors are ordered by particle number, then spin, with at most 5 sectors to one particle number; a site adds 0 to 2 particles, so join_in[b, 0] = b and every other entry is -1 or lies between b - 2 * 5 + 1 and b - 1.
All inputs are finite; a program needn't handle non-finite values.
Results may differ from a plain program's by a relative error of at most 0.0058.
Values may be sent and summed in bfloat16 or wider, within the bound.
No kernel may reach another device: no remote copies, remote signals or barrier semaphores. Data moves between devices by JAX's collectives and lax.ppermute only.
A program may use at most 128 MiB of HBM per device.

v0:
```python
import jax
import jax.numpy as jnp
from jax import lax
from jax.sharding import PartitionSpec as P

OWN = 8


def passed_along(value, axis, steps):
    count = lax.axis_size(axis)
    first, last = (max(0, -steps), min(count, count - steps))
    return lax.ppermute(value, axis, [(source, source + steps) for source in range(first, last)])


def shifted(value, axis, steps):
    count = lax.axis_size(axis)
    pairs = [(source, (source + steps) % count) for source in range(count)]
    return lax.ppermute(value, axis, pairs)


def neighbours(current):
    below_one = passed_along(current, "region", 1)
    below_two = passed_along(current[1:], "region", 2)
    return (below_one, below_two)


def advance(current, below_one, below_two, tensors, operator_blocks, join_in, block_sizes, base):
    slots = current.shape[0]
    tile = current.shape[1]
    chans = operator_blocks.shape[0]
    states = operator_blocks.shape[1]
    total = block_sizes.shape[0]
    pool = jnp.concatenate([below_two, below_one, current], axis=0)
    own_rows = lax.dynamic_slice_in_dim(join_in, base, slots, 0)
    own_sizes = lax.dynamic_slice_in_dim(block_sizes, base, slots, 0)
    valid = own_rows >= 0
    source = jnp.where(valid, own_rows, 0)
    offset = jnp.clip(own_rows - (base - 2 * slots + 1), 0, 3 * slots - 2)
    onehot = source[:, :, None] == jnp.arange(total, dtype=jnp.int32)[None, None, :]
    sizes_in = jnp.sum(jnp.where(onehot, block_sizes[None, None, :], 0), axis=-1)
    rows = jnp.arange(tile, dtype=jnp.int32)
    keep = (
        valid[:, :, None, None]
        & (rows[None, None, :, None] < sizes_in[:, :, None, None])
        & (rows[None, None, None, :] < own_sizes[:, None, None, None])
    )
    masked = jnp.where(keep, tensors, jnp.zeros_like(tensors))
    pieces = []
    for state_index in range(states):
        blocks = jnp.take(pool, offset[:, state_index], axis=0)
        left = jnp.einsum(
            "jxu,jxz->juz", masked[:, state_index], blocks, preferred_element_type=jnp.float32
        ).astype(jnp.bfloat16)
        left = left.reshape(slots, tile, chans, tile)
        mixed = jnp.einsum(
            "juwy,wk->juky",
            left,
            operator_blocks[:, state_index, :],
            preferred_element_type=jnp.float32,
        ).astype(jnp.bfloat16)
        pieces.append(mixed)
    stacked = jnp.stack(pieces, axis=1)
    result = jnp.einsum("jpuky,jpyv->jukv", stacked, masked, preferred_element_type=jnp.float32)
    return result.astype(jnp.bfloat16).reshape(slots, tile, chans * tile)


def per_device(environment, site_tensors, operator_blocks, join_in, block_sizes):
    slots = environment.shape[0]
    owner = lax.axis_index("region") % OWN
    base = owner * slots
    current = shifted(environment, "region", OWN)
    first_one, first_two = neighbours(current)
    current = advance(
        current,
        first_one,
        first_two,
        site_tensors[:, 0],
        operator_blocks,
        join_in,
        block_sizes,
        base,
    )
    return current


def solution(mesh):
    placed = (
        P(("groups", "region"), None, None),
        P(("groups", "region"), None, None, None, None),
        P(),
        P("groups", None),
        P("groups"),
    )
    return jax.shard_map(
        per_device,
        mesh=mesh,
        in_specs=placed,
        out_specs=P(("groups", "region"), None, None),
        check_vma=False,
    )
```

profile of v0, /device:TPU:25, one launch (start us, length us, event | category | flops | bytes accessed | tf_op | source)
XLA Modules:
  0.0 384.1 jit_solution(9605969055425498161)
XLA Ops:
  0.1 140.5 %collective-permute-done = bf16[5,96,3264]{2,1,0:T(8,128)(2,1)S(1)} collective-permute-done((bf16[5,96,3264]{2,1,0:T(8,128)(2,1)}, bf16[5,96,3264]{2,1,0:T(8,128)(2,1)S(1)}, u32[]{:S(2)}, u32[]{:S(2)}) %collective-permute-start) | collective-permute-done | bytes 3133472 | tf_op jit(solution)/shard_map/ppermute | solution.py:18
  140.6 3.5 collective-permute-start.2
  144.1 1.6 slice.61
  145.8 1.9 collective-permute-start.1
  148.8 2.0 copy.34
  151.0 2.1 and_select_fusion
  153.1 82.2 %collective-permute-done.1 = bf16[4,96,3264]{2,1,0:T(8,128)(2,1)} collective-permute-done((bf16[4,96,3264]{2,1,0:T(8,128)(2,1)}, bf16[4,96,3264]{2,1,0:T(8,128)(2,1)}, u32[]{:S(2)}, u32[]{:S(2)}) %collective-permute-start.1) | collective-permute-done | bytes 2506784 | tf_op jit(solution)/shard_map/ppermute | solution.py:12
  235.3 3.4 constant_dynamic-update-slice_fusion.2
  238.7 3.8 %constant_dynamic-update-slice_fusion.1 = bf16[14,96,3264]{2,1,0:T(8,128)(2,1)} fusion(bf16[14,96,3264]{2,1,0:T(8,128)(2,1)} %constant_dynamic-update-slice_fusion.2, bf16[5,96,3264]{2,1,0:T(8,128)(2,1)} %collective-permute-done.2), kind=kLoop, calls=%fused_computation.43 | loop fusion | bytes 6389760
  242.5 1.9 constant_dynamic-update-slice_fusion
  244.4 4.3 %gather_fusion.3 = bf16[5,96,3264]{2,1,0:T(8,128)(2,1)S(1)} fusion(bf16[14,96,3264]{2,1,0:T(8,128)(2,1)} %constant_dynamic-update-slice_fusion, s32[1024]{0:T(1024)S(1)} %get-tuple-element.27), kind=kCustom, calls=%fused_computation.3.clone | custom fusion | bytes 6266900 | tf_op jit(solution)/shard_map/jit(_take)/gather | solution.py:50
  248.7 3.6 convolution_convert_fusion
  252.4 5.9 %copy.44 = bf16[5,96,3264]{1,2,0:T(8,128)(2,1)} copy(bf16[5,96,3264]{2,1,0:T(8,128)(2,1)} %convolution_convert_fusion) | data formatting | bytes 6266880 | tf_op jit(solution)/shard_map/convert_element_type | solution.py:53
  258.2 9.3 %copy.46 = bf16[5,96,34,96]{3,2,1,0:T(8,128)(2,1)} copy(bf16[5,96,34,96]{1,3,2,0:T(8,128)(2,1)} %bitcast.96) | data formatting | bytes 6266880 | tf_op jit(solution)/shard_map/reshape | solution.py:54
  267.5 4.3 %gather_fusion.2 = bf16[5,96,3264]{2,1,0:T(8,128)(2,1)S(1)} fusion(bf16[14,96,3264]{2,1,0:T(8,128)(2,1)} %constant_dynamic-update-slice_fusion, s32[1024]{0:T(1024)S(1)} %get-tuple-element.28), kind=kCustom, calls=%fused_computation.2.clone | custom fusion | bytes 6266900 | tf_op jit(solution)/shard_map/jit(_take)/gather | solution.py:50
  271.8 3.6 convolution_convert_fusion.1
  275.4 5.9 %copy.41 = bf16[5,96,3264]{1,2,0:T(8,128)(2,1)} copy(bf16[5,96,3264]{2,1,0:T(8,128)(2,1)} %convolution_convert_fusion.1) | data formatting | bytes 6266880 | tf_op jit(solution)/shard_map/convert_element_type | solution.py:53
  281.3 9.3 %copy.43 = bf16[5,96,34,96]{3,2,1,0:T(8,128)(2,1)} copy(bf16[5,96,34,96]{1,3,2,0:T(8,128)(2,1)} %bitcast.97) | data formatting | bytes 6266880 | tf_op jit(solution)/shard_map/reshape | solution.py:54
  290.6 6.2 %gather_fusion.1 = bf16[5,96,3264]{2,1,0:T(8,128)(2,1)} fusion(bf16[14,96,3264]{2,1,0:T(8,128)(2,1)} %constant_dynamic-update-slice_fusion, s32[1024]{0:T(1024)S(1)} %get-tuple-element.29), kind=kCustom, calls=%fused_computation.1.clone | custom fusion | bytes 6266900 | tf_op jit(solution)/shard_map/jit(_take)/gather | solution.py:50
  296.8 4.3 %gather_fusion = bf16[5,96,3264]{2,1,0:T(8,128)(2,1)S(1)} fusion(bf16[14,96,3264]{2,1,0:T(8,128)(2,1)} %constant_dynamic-update-slice_fusion, s32[1024]{0:T(1024)S(1)} %get-tuple-element.30), kind=kCustom, calls=%fused_computation.clone | custom fusion | bytes 6266900 | tf_op jit(solution)/shard_map/jit(_take)/gather | solution.py:50
  301.1 4.7 %convolution_convert_fusion.2 = bf16[5,96,3264]{2,1,0:T(8,128)(2,1)} fusion(bf16[5,96,3264]{2,1,0:T(8,128)(2,1)} %gather_fusion.1, pred[5]{0:T(512)(128)(4,1)S(1)} %get-tuple-element.24, bf16[5,4,96,96]{2,3,0,1:T(8,128)(2,1)} %and_select_fusion), kind=kOutput, calls=%fused_computation.10 | convolution fusion | flops 303943680 | bytes 6451205 | tf_op jit(solution)/shard_map/jxu,jxz->juz/dot_general | solution.py:51
  305.7 5.9 %copy.38 = bf16[5,96,3264]{1,2,0:T(8,128)(2,1)} copy(bf16[5,96,3264]{2,1,0:T(8,128)(2,1)} %convolution_convert_fusion.2) | data formatting | bytes 6266880 | tf_op jit(solution)/shard_map/convert_element_type | solution.py:53
  311.6 9.3 %copy.40 = bf16[5,96,34,96]{3,2,1,0:T(8,128)(2,1)} copy(bf16[5,96,34,96]{1,3,2,0:T(8,128)(2,1)} %bitcast.98) | data formatting | bytes 6266880 | tf_op jit(solution)/shard_map/reshape | solution.py:54
  320.9 3.6 convolution_convert_fusion.3
  324.5 5.9 %copy.35 = bf16[5,96,3264]{1,2,0:T(8,128)(2,1)} copy(bf16[5,96,3264]{2,1,0:T(8,128)(2,1)} %convolution_convert_fusion.3) | data formatting | bytes 6266880 | tf_op jit(solution)/shard_map/convert_element_type | solution.py:53
  330.4 9.4 %copy.37 = bf16[5,96,34,96]{3,2,1,0:T(8,128)(2,1)} copy(bf16[5,96,34,96]{1,3,2,0:T(8,128)(2,1)} %bitcast.99) | data formatting | bytes 6266880 | tf_op jit(solution)/shard_map/reshape | solution.py:54
  339.8 4.0 %convert_bitcast_fusion = bf16[5,1,96,34,96]{4,3,2,0,1:T(8,128)(2,1)S(1)} fusion(bf16[5,96,34,96]{3,2,1,0:T(8,128)(2,1)} %copy.46, bf16[34,1,34]{0,2,1:T(8,128)(2,1)S(1)} %copy.62), kind=kOutput, calls=%fused_computation.12 | convolution fusion | flops 108103680 | bytes 6269192 | tf_op jit(solution)/shard_map/juwy,wk->juky/dot_general | solution.py:55
  346.7 1.4 convert_bitcast_fusion.3
  348.2 9.8 %pad_maximum_fusion = bf16[5,4,96,34,96]{4,3,2,0,1:T(8,128)(2,1)} fusion(bf16[5,1,96,34,96]{4,3,2,0,1:T(8,128)(2,1)S(1)} %convert_bitcast_fusion, bf16[5,1,96,34,96]{4,3,2,0,1:T(8,128)(2,1)S(1)} %convert_bitcast_fusion.1, bf16[5,1,96,34,96]{4,3,2,0,1:T(8,128)(2,1)S(1)} %convert_bitcast_fusion.2, bf16[5,1,96,34,96]{4,3,2,0,1:T(8,128)(2,1)S(1)} %convert_bitcast_fusion.3), kind=kLoop, calls=%fused_computation.4 | loop fusion | flops 18800640 | bytes 25067520 | tf_op jit(solution)/shard_map/stack | solution.py:62
  358.0 13.8 %bitcast_convert_fusion = bf16[5,96,34,96]{3,1,2,0:T(8,128)(2,1)} fusion(bf16[5,4,96,34,96]{4,3,2,0,1:T(8,128)(2,1)} %pad_maximum_fusion, bf16[5,1,4,96,96]{3,4,0,2,1:T(8,128)(2,1)S(1)} %copy-done, pred[5,96]{1,0:T(8,128)(4,1)S(1)} %iota_compare_fusion.2, pred[5,4,96]{2,0,1:T(8,128)(4,1)S(1)} %fusion.17), kind=kOutput, calls=%fused_computation.7 | convolution fusion | flops 1205176320 | bytes 16038240 | tf_op jit(solution)/shard_map/jpuky,jpyv->jukv/dot_general | solution.py:63
  371.8 6.4 %copy.49 = bf16[5,96,34,96]{1,3,2,0:T(8,128)(2,1)} copy(bf16[5,96,34,96]{3,1,2,0:T(8,128)(2,1)} %bitcast_convert_fusion) | data formatting | bytes 6266880 | tf_op jit(solution)/shard_map/convert_element_type | solution.py:64
  378.1 6.0 %copy.50 = bf16[5,96,3264]{2,1,0:T(8,128)(2,1)} copy(bf16[5,96,3264]{1,2,0:T(8,128)(2,1)} %bitcast.100) | data formatting | bytes 6266880 | tf_op jit(solution)/shard_map/reshape | solution.py:64
  (42 shorter events, 4.2 us)
Async XLA Ops:
  0.0 147.7 %copy-start.3 = (s32[40]{0:T(128)S(1)}, s32[40]{0:T(128)}, u32[]{:S(2)}) copy-start(s32[40]{0:T(128)} %param.11) | copy-start | bytes 484
  0.0 147.8 %copy-start.2 = (s32[40,4]{0,1:T(4,128)S(1)}, s32[40,4]{0,1:T(4,128)}, u32[]{:S(2)}) copy-start(s32[40,4]{0,1:T(4,128)} %param.10) | copy-start | bytes 1924
  0.0 148.3 %copy-start.1 = (bf16[34,4,34]{2,1,0:T(4,128)(2,1)S(1)}, bf16[34,4,34]{2,1,0:T(4,128)(2,1)}, u32[]{:S(2)}) copy-start(bf16[34,4,34]{2,1,0:T(4,128)(2,1)} %param.9) | copy-start | bytes 27748
  0.0 140.6 %collective-permute-start = (bf16[5,96,3264]{2,1,0:T(8,128)(2,1)}, bf16[5,96,3264]{2,1,0:T(8,128)(2,1)S(1)}, u32[]{:S(2)}, u32[]{:S(2)}) collective-permute-start(bf16[5,96,3264]{2,1,0:T(8,128)(2,1)} %param.7), channel_id=1, source_target_pairs={{0,8},{1,9},{2,10},{3,11},{4,12},{5,13},{6,14},{7,15},{8,0},{9,1},... | collective-permute-start | bytes 9400328 | tf_op jit(solution)/shard_map/ppermute | solution.py:18
  140.6 98.1 %collective-permute-start.2 = (bf16[5,96,3264]{2,1,0:T(8,128)(2,1)S(1)}, bf16[5,96,3264]{2,1,0:T(8,128)(2,1)}, u32[]{:S(2)}, u32[]{:S(2)}) collective-permute-start(bf16[5,96,3264]{2,1,0:T(8,128)(2,1)S(1)} %collective-permute-done), channel_id=1, source_target_pairs={{0,1},{1,2},{2,3},{3,4},{4,5},{5,6},{6,7},{7,8},{8,9},{9,10},{10,1... | collective-permute-start | bytes 9400328 | tf_op jit(solution)/shard_map/ppermute | solution.py:12
  145.8 89.5 %collective-permute-start.1 = (bf16[4,96,3264]{2,1,0:T(8,128)(2,1)}, bf16[4,96,3264]{2,1,0:T(8,128)(2,1)}, u32[]{:S(2)}, u32[]{:S(2)}) collective-permute-start(bf16[4,96,3264]{2,1,0:T(8,128)(2,1)} %slice.61), channel_id=1, source_target_pairs={{0,2},{1,3},{2,4},{3,5},{4,6},{5,7},{6,8},{7,9},{8,10},{9,11},{10,... | collective-permute-start | bytes 7520264 | tf_op jit(solution)/shard_map/ppermute | solution.py:12
  330.4 13.3 %slice-start = ((s8[4915200]{0:T(1024)(128)(4,1)}), s8[720896]{0:T(1024)(128)(4,1)S(1)}, s32[]{:S(2)}) async-start(s8[4915200]{0:T(1024)(128)(4,1)} %bitcast.90), calls=%async_computation | async-start | bytes 1441792
  339.8 4.0 %slice-start.1 = ((s8[4915200]{0:T(1024)(128)(4,1)}), s8[4194304]{0:T(1024)(128)(4,1)S(1)}, s32[]{:S(2)}) async-start(s8[4915200]{0:T(1024)(128)(4,1)} %bitcast.90), calls=%async_computation.1 | async-start | bytes 8388608
  339.8 5.4 %slice-start.2 = ((s8[4915200]{0:T(1024)(128)(4,1)}), s8[4194304]{0:T(1024)(128)(4,1)S(1)}, s32[]{:S(2)}) async-start(s8[4915200]{0:T(1024)(128)(4,1)} %bitcast.92), calls=%async_computation.2 | async-start | bytes 8388608
  343.8 1.5 slice-start.3
  343.8 2.9 slice-start.4
  345.3 1.4 slice-start.5
  348.1 9.8 %copy-start = (bf16[5,1,4,96,96]{3,4,0,2,1:T(8,128)(2,1)S(1)}, bf16[5,1,4,96,96]{3,4,0,2,1:T(8,128)(2,1)}, u32[]{:S(2)}) copy-start(bf16[5,1,4,96,96]{3,4,0,2,1:T(8,128)(2,1)} %copy.34) | copy-start | bytes 1105924
where the time goes:
time: 386 us; the launch traced here: 384 us
  waiting for transfers between devices  223 us (58%)
  local copies, waits for them, and re-layouts  106 us (27%)
  matrix products  37.6 us (10%)
  other arithmetic  12.4 us (3%)
  starting transfers between devices  5.55 us (1%)
    ppermute x1, waiting for transfers between devices, shifted(): return lax.ppermute(value, axis, pairs)  140 us
    ppermute x2, waiting for transfers between devices, passed_along(): lax.ppermute(value, axis, [(source, source + steps) for source in range(f...  82.2 us
    reshape x4, local copies, waits for them, and re-layouts, advance(): left = left.reshape(slots, tile, chans, tile)  37.2 us
    convert_element_type x4, local copies, waits for them, and re-layouts, advance(): left = jnp.einsum('jxu,jxz->juz', masked[:, state_index], blocks, preferr...  23.5 us
    gather x4, local copies, waits for them, and re-layouts, advance(): blocks = jnp.take(pool, offset[:, state_index], axis=0)  19 us
    dot_general x4, matrix products, advance(): jnp.einsum('jxu,jxz->juz', masked[:, state_index], blocks, preferred_elem...  15.6 us
    dot_general x1, matrix products, advance(): jnp.einsum('jpuky,jpyv->jukv', stacked, masked, preferred_element_type=jn...  13.8 us
    another operation x1, other arithmetic, advance(): stacked = jnp.stack(pieces, axis=1)  9.82 us
  transfers between devices with their start and end apart: 3, of which 2 were waited for; matrix products, arithmetic and copies ran while one was open for 3% of the time, Pallas kernels for 0%

commit v1 on v0

v1 whole, which is shorter than its diff:
```python
import functools

import jax
import jax.numpy as jnp
from jax import lax
from jax.experimental import pallas as pl
from jax.experimental.pallas import tpu as pltpu
from jax.sharding import PartitionSpec as P

OWN = 8
LANES = 128
ROWS = 40
GROUP = 6


def shifted(value, axis, steps):
    count = lax.axis_size(axis)
    return lax.ppermute(value, axis, [(source, (source + steps) % count) for source in range(count)])


def to_next(value, axis, first):
    count = lax.axis_size(axis)
    pairs = [(source, source + 1) for source in range(count) if first <= source % OWN < OWN - 1]
    return lax.ppermute(value, axis, pairs)


def stage_kernel(first, last, blocks, offs, *refs):
    block_refs = refs[:blocks]
    gt_ref, gy_ref, mix_ref = refs[blocks : blocks + 3]
    acc_in = None if first else refs[blocks + 3]
    result, slab, yf, *rest = refs[blocks + 3 + (not first) :]
    tile = gt_ref.shape[-1]
    states = mix_ref.shape[0]
    chans = block_refs[0].shape[-1] // tile
    span = GROUP * ROWS
    b = pl.program_id(0)
    acc = rest[0] if last else result.at[0]

    @pl.when(b == 0)
    def _():
        yf[...] = jnp.zeros_like(yf)
        pad = jnp.zeros((tile, LANES - tile), jnp.bfloat16)
        place = 0
        for ref in block_refs:
            for i in range(ref.shape[0]):
                for w in range(chans):
                    piece = ref[i, :, w * tile : (w + 1) * tile]
                    slab[place, :, w * LANES : (w + 1) * LANES] = jnp.concatenate([piece, pad], axis=1)
                place += 1

    acc[...] = jnp.zeros(acc.shape, jnp.float32) if first else acc_in[0]
    for q in range(states):
        a = offs[b, q]

        @pl.when(a >= 0)
        def _():
            for c in range(0, chans, 2):
                y = jnp.dot(gt_ref[0, q], slab[a, :, c * LANES : (c + 2) * LANES], preferred_element_type=jnp.float32)
                yf[pl.ds(c, tile, stride=ROWS), :] = y[:, :LANES]
                yf[pl.ds(c + 1, tile, stride=ROWS), :] = y[:, LANES:]
            for g in range(0, tile // GROUP, 2):
                one, two = (slice((g + k) * span, (g + k + 1) * span) for k in range(2))
                rhs = jnp.concatenate([yf[one, :].astype(jnp.bfloat16), yf[two, :].astype(jnp.bfloat16)], axis=1)
                v = jnp.dot(mix_ref[q], rhs, preferred_element_type=jnp.float32).astype(jnp.bfloat16)
                acc[one, :] += jnp.dot(v[:, :LANES], gy_ref[0, q], preferred_element_type=jnp.float32)
                acc[two, :] += jnp.dot(v[:, LANES:], gy_ref[0, q], preferred_element_type=jnp.float32)

    if last:
        for w in range(chans):
            done = acc[pl.ds(w, tile, stride=ROWS), :].astype(jnp.bfloat16)
            result[0, :, w * tile : (w + 1) * tile] = done[:, :tile]


def stage(offs, arrays, gt, gy, mix, acc, last, chans):
    slots, states, tile, _ = gt.shape
    first = acc is None
    total = sum(a.shape[0] for a in arrays)
    full = tile * ROWS

    def whole(a):
        return pl.BlockSpec(a.shape, lambda b, offs: (0,) * a.ndim)

    def one(a):
        return pl.BlockSpec((1,) + a.shape[1:], lambda b, offs: (b,) + (0,) * (a.ndim - 1))

    args = list(arrays) + [gt, gy, mix]
    specs = [whole(a) for a in arrays] + [one(gt), one(gy), whole(mix)]
    if not first:
        args.append(acc)
        specs.append(one(acc))
    if last:
        out = jax.ShapeDtypeStruct((slots, tile, chans * tile), jnp.bfloat16)
    else:
        out = jax.ShapeDtypeStruct((slots, full, LANES), jnp.float32)
    scratch = [pltpu.VMEM((total, tile, chans * LANES), jnp.bfloat16), pltpu.VMEM((full, LANES), jnp.float32)]
    if last:
        scratch.append(pltpu.VMEM((full, LANES), jnp.float32))
    aliases = {} if first or last else {len(args): 0}
    flops = 2 * slots * states * tile * tile * chans * (2 * tile + chans) * total // (3 * slots)
    return pl.pallas_call(
        functools.partial(stage_kernel, first, last, len(arrays)),
        out_shape=out,
        grid_spec=pltpu.PrefetchScalarGridSpec(
            num_scalar_prefetch=1, grid=(slots,), in_specs=specs, out_specs=one(out), scratch_shapes=scratch
        ),
        input_output_aliases=aliases,
        compiler_params=pltpu.CompilerParams(vmem_limit_bytes=40 * 1024 * 1024),
        cost_estimate=pl.CostEstimate(flops=flops * 8, bytes_accessed=8 * 1024 * 1024, transcendentals=0),
    )(offs, *args)


def tied(value, after):
    return lax.optimization_barrier((value, after))[0]


def per_device(environment, site_tensors, operator_blocks, join_in, block_sizes):
    slots, tile, _ = environment.shape
    chans, states, _ = operator_blocks.shape
    base = (lax.axis_index("region") % OWN) * slots

    order = list(reversed(range(slots)))
    received = {}
    for place, slot in enumerate(order):
        block = environment[slot : slot + 1]
        if place >= 2:
            block = tied(block, received[order[place - 2]])
        received[slot] = shifted(block, "region", OWN)

    tensors = site_tensors[:, 0]
    own_rows = lax.dynamic_slice_in_dim(join_in, base, slots, 0)
    own_sizes = lax.dynamic_slice_in_dim(block_sizes, base, slots, 0)
    valid = own_rows >= 0
    sizes_in = jnp.take(block_sizes, jnp.where(valid, own_rows, 0), axis=0)
    rows = jnp.arange(tile, dtype=jnp.int32)
    keep = (
        valid[:, :, None, None]
        & (rows[None, None, :, None] < sizes_in[:, :, None, None])
        & (rows[None, None, None, :] < own_sizes[:, None, None, None])
    )
    masked = jnp.where(keep, tensors, jnp.zeros_like(tensors))
    gt = jnp.swapaxes(masked, 2, 3)
    gy = jnp.pad(masked, ((0, 0), (0, 0), (0, LANES - tile), (0, LANES - tile)))
    ops = jnp.pad(jnp.transpose(operator_blocks, (1, 2, 0)), ((0, 0), (0, ROWS - chans), (0, ROWS - chans)))
    mix = jnp.einsum("gh,qkw->qgkhw", jnp.eye(GROUP, dtype=ops.dtype), ops)
    mix = mix.reshape(states, GROUP * ROWS, GROUP * ROWS)

    place = own_rows - base + 2 * slots
    hop = 2 - place // slots
    slot_of = place % slots
    groups = [order[i : i + 2] for i in range(0, slots, 2)]
    acc = None
    for number, group in enumerate(groups):
        last = number == len(groups) - 1
        here = jnp.concatenate([received[slot] for slot in group], axis=0)
        one = to_next(here, "region", 0)
        arrays = [here, one]
        if group != [0]:
            arrays.append(to_next(one, "region", 1))
        count = len(group)
        index = group[0] - slot_of
        mine = valid & (index >= 0) & (index < count)
        offs = jnp.where(mine, hop * count + index, -1).astype(jnp.int32)
        acc = stage(offs, arrays, gt, gy, mix, acc, last, chans)
    return acc


def solution(mesh):
    placed = (
        P(("groups", "region"), None, None),
        P(("groups", "region"), None, None, None, None),
        P(),
        P("groups", None),
        P("groups"),
    )
    return jax.shard_map(
        per_device,
        mesh=mesh,
        in_specs=placed,
        out_specs=P(("groups", "region"), None, None),
        check_vma=False,
    )
```

time: 386 us -> 229 us (0.59)
  the two profiles are of different devices: /device:TPU:25 before, /device:TPU:24 now
where the time goes in v1:
time: 229 us; the launch traced here: 228 us
  waiting for transfers between devices  140 us (61%)
  Pallas kernels  59.2 us (26%)
  local copies, waits for them, and re-layouts  14 us (6%)
  starting transfers between devices  12.9 us (6%)
  other arithmetic  2.33 us (1%)
    ppermute x5, waiting for transfers between devices, shifted(): lax.ppermute(value, axis, [(source, (source + steps) % count) for source...  106 us
    pallas_call x3, Pallas kernels, stage(): pl.pallas_call(functools.partial(stage_kernel, first, last, len(arrays)),...  59.2 us
    ppermute x5, waiting for transfers between devices, to_next(): return lax.ppermute(value, axis, pairs)  33.2 us
    ppermute x5, starting transfers between devices, to_next(): return lax.ppermute(value, axis, pairs)  9.87 us
    unnamed x28, local copies, waits for them, and re-layouts  6.68 us
  transfers between devices with their start and end apart: 10, of which 6 were waited for; matrix products, arithmetic and copies ran while one was open for 4% of the time, Pallas kernels for 21%

profile of v1, /device:TPU:24, one launch (start us, length us, event | category | flops | bytes accessed | tf_op | source)
XLA Modules:
  0.0 228.1 jit_solution(7036342660089746771)
XLA Ops:
  0.0 2.9 %fusion.4 = (bf16[1,96,3264]{2,1,0:T(8,128)(2,1)S(1)}, bf16[1,96,3264]{2,1,0:T(8,128)(2,1)S(1)}, bf16[1,96,3264]{2,1,0:T(8,128)(2,1)S(1)}, bf16[1,96,3264]{2,1,0:T(8,128)(2,1)}, bf16[1,96,3264]{2,1,0:T(8,128)(2,1)S(1)}) fusion(bf16[5,96,3264]{2,1,0:T(8,128)(2,1)} %param.5), kind=kLoop, calls=%fused_computation.27 | loop fusion | bytes 6266880 | tf_op jit(solution)/shard_map/slice | solution.py:124
  2.9 0.3 collective-permute-start.4
  3.3 2.6 %collective-permute-start = (bf16[1,96,3264]{2,1,0:T(8,128)(2,1)S(1)}, bf16[1,96,3264]{2,1,0:T(8,128)(2,1)}, u32[]{:S(2)}, u32[]{:S(2)}) collective-permute-start(bf16[1,96,3264]{2,1,0:T(8,128)(2,1)S(1)} %get-tuple-element.14), channel_id=1, source_target_pairs={{0,8},{1,9},{2,10},{3,11},{4,12},{5,13},{6,14},{7,15},{8,0},{9,1},... | collective-permute-start | bytes 1880072 | tf_op jit(solution)/shard_map/ppermute | solution.py:18
  6.0 0.1 copy.17
  6.1 41.2 %collective-permute-done.4 = bf16[1,96,3264]{2,1,0:T(8,128)(2,1)S(1)} collective-permute-done((bf16[1,96,3264]{2,1,0:T(8,128)(2,1)S(1)}, bf16[1,96,3264]{2,1,0:T(8,128)(2,1)S(1)}, u32[]{:S(2)}, u32[]{:S(2)}) %collective-permute-start.4) | collective-permute-done | bytes 626720 | tf_op jit(solution)/shard_map/ppermute | solution.py:18
  47.3 27.5 %collective-permute-done = bf16[1,96,3264]{2,1,0:T(8,128)(2,1)} collective-permute-done((bf16[1,96,3264]{2,1,0:T(8,128)(2,1)S(1)}, bf16[1,96,3264]{2,1,0:T(8,128)(2,1)}, u32[]{:S(2)}, u32[]{:S(2)}) %collective-permute-start) | collective-permute-done | bytes 626720 | tf_op jit(solution)/shard_map/ppermute | solution.py:18
  74.8 1.2 constant_dynamic-update-slice_fusion.3
  76.0 0.1 copy-done.10
  76.1 1.9 collective-permute-start.8
  78.1 37.6 %collective-permute-done.1 = bf16[1,96,3264]{2,1,0:T(8,128)(2,1)S(1)} collective-permute-done((bf16[1,96,3264]{2,1,0:T(8,128)(2,1)S(1)}, bf16[1,96,3264]{2,1,0:T(8,128)(2,1)S(1)}, u32[]{:S(2)}, u32[]{:S(2)}) %collective-permute-start.1) | collective-permute-done | bytes 626720 | tf_op jit(solution)/shard_map/ppermute | solution.py:18
  115.8 2.0 collective-permute-start.6
  117.9 0.1 reshape.48
  118.0 0.7 gather_fusion
  118.8 4.0 %collective-permute-done.8.refs_1_ = bf16[2,96,3264]{2,1,0:T(8,128)(2,1)} collective-permute-done((bf16[2,96,3264]{2,1,0:T(8,128)(2,1)S(1)}, bf16[2,96,3264]{2,1,0:T(8,128)(2,1)}, u32[]{:S(2)}, u32[]{:S(2)}) %collective-permute-start.8) | collective-permute-done | bytes 1253408 | tf_op jit(solution)/shard_map/ppermute | solution.py:24
  122.7 1.9 collective-permute-start.9
  124.7 0.1 fusion
  124.8 0.3 fusion.5
  125.2 24.9 %collective-permute-done.6.refs_1_ = bf16[2,96,3264]{2,1,0:T(8,128)(2,1)} collective-permute-done((bf16[2,96,3264]{2,1,0:T(8,128)(2,1)S(1)}, bf16[2,96,3264]{2,1,0:T(8,128)(2,1)}, u32[]{:S(2)}, u32[]{:S(2)}) %collective-permute-start.6) | collective-permute-done | bytes 1253408 | tf_op jit(solution)/shard_map/ppermute | solution.py:24
  150.1 1.9 collective-permute-start.7
  152.0 0.3 and_select_fusion
  152.4 0.1 copy.18
  152.5 0.3 copy.16.refs_3_.refs_2_
  152.8 0.2 pad.8.refs_4_.refs_3_
  153.0 1.5 multiply_bitcast_fusion
  154.5 2.8 %reshape.45.refs_5_.refs_4_ = bf16[4,240,240]{2,1,0:T(8,128)(2,1)S(1)} reshape(bf16[4,6,40,6,40]{4,3,2,1,0:T(8,128)(2,1)} %multiply_bitcast_fusion) | data formatting | bytes 921600 | tf_op jit(solution)/shard_map/reshape | solution.py:145
  157.3 2.1 collective-permute-start.3
  159.4 4.4 %collective-permute-done.9.refs_2_ = bf16[2,96,3264]{2,1,0:T(8,128)(2,1)} collective-permute-done((bf16[2,96,3264]{2,1,0:T(8,128)(2,1)}, bf16[2,96,3264]{2,1,0:T(8,128)(2,1)}, u32[]{:S(2)}, u32[]{:S(2)}) %collective-permute-start.9) | collective-permute-done | bytes 1253408 | tf_op jit(solution)/shard_map/ppermute | solution.py:24
  163.8 1.3 copy-done.5
  165.1 26.1 %shard_map.55.refs_6_ = f32[5,3840,128]{2,1,0:T(8,128)} custom-call(s32[5,4]{1,0:T(8,128)S(1)} %get-tuple-element.11.offs, bf16[2,96,3264]{2,1,0:T(8,128)(2,1)S(1)} %copy-done.5, bf16[2,96,3264]{2,1,0:T(8,128)(2,1)} %collective-permute-done.8.refs_1_, bf16[2,96,3264]{2,1,0:T(8,128)(2,1)} %collective-permute-done.9.refs_2_, ...), custom_call_target="tpu_custom_call" | custom-call | flops 9064415232 | bytes 8388608 | tf_op jit(solution)/shard_map/pallas_call | solution.py:100
  191.3 21.0 %shard_map.56.refs_5_ = f32[5,3840,128]{2,1,0:T(8,128)} custom-call(s32[5,4]{1,0:T(8,128)S(1)} %get-tuple-element.18.offs, bf16[2,96,3264]{2,1,0:T(8,128)(2,1)S(1)} %copy-done.3, bf16[2,96,3264]{2,1,0:T(8,128)(2,1)} %collective-permute-done.6.refs_1_, bf16[2,96,3264]{2,1,0:T(8,128)(2,1)} %collective-permute-done.7.refs_2_, ...), custom_call_target="tpu_custom_call", output_to_operand_aliasing={{}: (7, {})} | custom-call | flops 9064415232 | bytes 8388608 | tf_op jit(solution)/shard_map/pallas_call | solution.py:100
  212.3 3.8 %copy-done.1 = f32[5,3840,128]{2,1,0:T(8,128)S(1)} copy-done((f32[5,3840,128]{2,1,0:T(8,128)S(1)}, f32[5,3840,128]{2,1,0:T(8,128)}, u32[]{:S(2)}) %copy-start.1) | copy-done | bytes 9830424
  216.1 12.1 %shard_map.57 = bf16[5,96,3264]{2,1,0:T(8,128)(2,1)} custom-call(s32[5,4]{1,0:T(8,128)S(1)} %get-tuple-element.20.offs, bf16[1,96,3264]{2,1,0:T(8,128)(2,1)S(1)} %collective-permute-done.2.refs_0_, bf16[1,96,3264]{2,1,0:T(8,128)(2,1)S(1)} %collective-permute-done.3.refs_1_, bf16[5,4,96,96]{3,2,1,0:T(8,128)(2,1)S(1)} %copy.16.refs_3_.refs_2_, ...), custom_call_target="tpu_custom_call" | custom-call | flops 3021471744 | bytes 8388608 | tf_op jit(solution)/shard_map/pallas_call | solution.py:100
  (41 shorter events, 0.6 us)
Async XLA Ops:
  0.0 5.9 %copy-start = (s32[40,4]{0,1:T(4,128)S(1)}, s32[40,4]{0,1:T(4,128)}, u32[]{:S(2)}) copy-start(s32[40,4]{0,1:T(4,128)} %param.8) | copy-start | bytes 1924
  0.0 5.8 %copy-start.6 = (s32[40]{0:T(128)S(1)}, s32[40]{0:T(128)}, u32[]{:S(2)}) copy-start(s32[40]{0:T(128)} %param.9) | copy-start | bytes 484
  2.9 44.4 %collective-permute-start.4 = (bf16[1,96,3264]{2,1,0:T(8,128)(2,1)S(1)}, bf16[1,96,3264]{2,1,0:T(8,128)(2,1)S(1)}, u32[]{:S(2)}, u32[]{:S(2)}) collective-permute-start(bf16[1,96,3264]{2,1,0:T(8,128)(2,1)S(1)} %get-tuple-element.13), channel_id=1, source_target_pairs={{0,8},{1,9},{2,10},{3,11},{4,12},{5,13},{6,14},{7,15},{8,0},{9,1},... | collective-permute-start | bytes 1880072 | tf_op jit(solution)/shard_map/ppermute | solution.py:18
  3.3 71.5 %collective-permute-start = (bf16[1,96,3264]{2,1,0:T(8,128)(2,1)S(1)}, bf16[1,96,3264]{2,1,0:T(8,128)(2,1)}, u32[]{:S(2)}, u32[]{:S(2)}) collective-permute-start(bf16[1,96,3264]{2,1,0:T(8,128)(2,1)S(1)} %get-tuple-element.14), channel_id=1, source_target_pairs={{0,8},{1,9},{2,10},{3,11},{4,12},{5,13},{6,14},{7,15},{8,0},{9,1},... | collective-permute-start | bytes 1880072 | tf_op jit(solution)/shard_map/ppermute | solution.py:18
  47.3 27.5 %copy-start.9 = (bf16[1,96,3264]{2,1,0:T(8,128)(2,1)}, bf16[1,96,3264]{2,1,0:T(8,128)(2,1)S(1)}, u32[]{:S(2)}) copy-start(bf16[1,96,3264]{2,1,0:T(8,128)(2,1)S(1)} %collective-permute-done.4) | copy-start | bytes 1880068
  47.3 68.4 %collective-permute-start.5 = (bf16[1,96,3264]{2,1,0:T(8,128)(2,1)S(1)}, bf16[1,96,3264]{2,1,0:T(8,128)(2,1)S(1)}, u32[]{:S(2)}, u32[]{:S(2)}) collective-permute-start(bf16[1,96,3264]{2,1,0:T(8,128)(2,1)S(1)} %get-tuple-element.10), channel_id=1, source_target_pairs={{0,8},{1,9},{2,10},{3,11},{4,12},{5,13},{6,14},{7,15},{8,0},{9,1},... | collective-permute-start | bytes 1880072 | tf_op jit(solution)/shard_map/ppermute | solution.py:18
  74.8 40.9 %collective-permute-start.1 = (bf16[1,96,3264]{2,1,0:T(8,128)(2,1)S(1)}, bf16[1,96,3264]{2,1,0:T(8,128)(2,1)S(1)}, u32[]{:S(2)}, u32[]{:S(2)}) collective-permute-start(bf16[1,96,3264]{2,1,0:T(8,128)(2,1)S(1)} %get-tuple-element.8), channel_id=1, source_target_pairs={{0,8},{1,9},{2,10},{3,11},{4,12},{5,13},{6,14},{7,15},{8,0},{9,1},... | collective-permute-start | bytes 1880072 | tf_op jit(solution)/shard_map/ppermute | solution.py:18
  74.8 1.3 copy-start.10
  76.1 39.7 %copy-start.4 = (bf16[2,96,3264]{2,1,0:T(8,128)(2,1)}, bf16[2,96,3264]{2,1,0:T(8,128)(2,1)S(1)}, u32[]{:S(2)}) copy-start(bf16[2,96,3264]{2,1,0:T(8,128)(2,1)S(1)} %constant_dynamic-update-slice_fusion.2.refs_0_) | copy-start | bytes 3760132
  76.1 46.6 %collective-permute-start.8 = (bf16[2,96,3264]{2,1,0:T(8,128)(2,1)S(1)}, bf16[2,96,3264]{2,1,0:T(8,128)(2,1)}, u32[]{:S(2)}, u32[]{:S(2)}) collective-permute-start(bf16[2,96,3264]{2,1,0:T(8,128)(2,1)S(1)} %constant_dynamic-update-slice_fusion.2.refs_0_), channel_id=1, source_target_pairs={{0,1},{1,2},{2,3},{3,4},{4,5},{5,6},{6,7},{8,9},{9,10},{10,11},{11... | collective-permute-start | bytes 3760136 | tf_op jit(solution)/shard_map/ppermute | solution.py:24
  115.8 2.9 %copy-start.2 = (bf16[2,96,3264]{2,1,0:T(8,128)(2,1)}, bf16[2,96,3264]{2,1,0:T(8,128)(2,1)S(1)}, u32[]{:S(2)}) copy-start(bf16[2,96,3264]{2,1,0:T(8,128)(2,1)S(1)} %constant_dynamic-update-slice_fusion.refs_0_) | copy-start | bytes 3760132
  115.8 34.3 %collective-permute-start.6 = (bf16[2,96,3264]{2,1,0:T(8,128)(2,1)S(1)}, bf16[2,96,3264]{2,1,0:T(8,128)(2,1)}, u32[]{:S(2)}, u32[]{:S(2)}) collective-permute-start(bf16[2,96,3264]{2,1,0:T(8,128)(2,1)S(1)} %constant_dynamic-update-slice_fusion.refs_0_), channel_id=1, source_target_pairs={{0,1},{1,2},{2,3},{3,4},{4,5},{5,6},{6,7},{8,9},{9,10},{10,11},{11... | collective-permute-start | bytes 3760136 | tf_op jit(solution)/shard_map/ppermute | solution.py:24
  118.0 6.8 %copy-start.7 = (bf16[5,1,4,96,96]{4,3,2,1,0:T(8,128)(2,1)S(1)}, bf16[5,1,4,96,96]{4,3,2,1,0:T(8,128)(2,1)}, u32[]{:S(2)}) copy-start(bf16[5,1,4,96,96]{4,3,2,1,0:T(8,128)(2,1)} %param.6) | copy-start | bytes 1105924
  118.7 33.7 %copy-start.11 = (bf16[34,4,34]{2,1,0:T(4,128)(2,1)S(1)}, bf16[34,4,34]{2,1,0:T(4,128)(2,1)}, u32[]{:S(2)}) copy-start(bf16[34,4,34]{2,1,0:T(4,128)(2,1)} %param.7) | copy-start | bytes 27748
  118.8 33.3 %copy-start.8 = (bf16[5,1,4,96,96]{4,3,2,1,0:T(8,128)(2,1)S(1)}, bf16[5,1,4,96,96]{4,3,2,1,0:T(8,128)(2,1)}, u32[]{:S(2)}) copy-start(bf16[5,1,4,96,96]{4,3,2,1,0:T(8,128)(2,1)} %param.6) | copy-start | bytes 1105924
  122.7 41.1 %collective-permute-start.9 = (bf16[2,96,3264]{2,1,0:T(8,128)(2,1)}, bf16[2,96,3264]{2,1,0:T(8,128)(2,1)}, u32[]{:S(2)}, u32[]{:S(2)}) collective-permute-start(bf16[2,96,3264]{2,1,0:T(8,128)(2,1)} %collective-permute-done.8.refs_1_), channel_id=1, source_target_pairs={{1,2},{2,3},{3,4},{4,5},{5,6},{6,7},{9,10},{10,11},{11,12},{12,13}... | collective-permute-start | bytes 3760136 | tf_op jit(solution)/shard_map/ppermute | solution.py:24
  125.1 32.2 %collective-permute-start.2 = (bf16[1,96,3264]{2,1,0:T(8,128)(2,1)}, bf16[1,96,3264]{2,1,0:T(8,128)(2,1)S(1)}, u32[]{:S(2)}, u32[]{:S(2)}) collective-permute-start(bf16[1,96,3264]{2,1,0:T(8,128)(2,1)} %get-tuple-element.9), channel_id=1, source_target_pairs={{0,8},{1,9},{2,10},{3,11},{4,12},{5,13},{6,14},{7,15},{8,0},{9,1},... | collective-permute-start | bytes 1880072 | tf_op jit(solution)/shard_map/ppermute | solution.py:18
  150.1 41.1 %collective-permute-start.7 = (bf16[2,96,3264]{2,1,0:T(8,128)(2,1)}, bf16[2,96,3264]{2,1,0:T(8,128)(2,1)}, u32[]{:S(2)}, u32[]{:S(2)}) collective-permute-start(bf16[2,96,3264]{2,1,0:T(8,128)(2,1)} %collective-permute-done.6.refs_1_), channel_id=1, source_target_pairs={{1,2},{2,3},{3,4},{4,5},{5,6},{6,7},{9,10},{10,11},{11,12},{12,13}... | collective-permute-start | bytes 3760136 | tf_op jit(solution)/shard_map/ppermute | solution.py:24
  157.3 55.0 %collective-permute-start.3 = (bf16[1,96,3264]{2,1,0:T(8,128)(2,1)S(1)}, bf16[1,96,3264]{2,1,0:T(8,128)(2,1)S(1)}, u32[]{:S(2)}, u32[]{:S(2)}) collective-permute-start(bf16[1,96,3264]{2,1,0:T(8,128)(2,1)S(1)} %collective-permute-done.2.refs_0_), channel_id=1, source_target_pairs={{0,1},{1,2},{2,3},{3,4},{4,5},{5,6},{6,7},{8,9},{9,10},{10,11},{11... | collective-permute-start | bytes 1880072 | tf_op jit(solution)/shard_map/ppermute | solution.py:24
  163.8 1.3 copy-start.5
  165.1 26.1 %copy-start.3 = (bf16[2,96,3264]{2,1,0:T(8,128)(2,1)S(1)}, bf16[2,96,3264]{2,1,0:T(8,128)(2,1)}, u32[]{:S(2)}) copy-start(bf16[2,96,3264]{2,1,0:T(8,128)(2,1)} %copy-done.2) | copy-start | bytes 3760132
  212.3 3.8 %copy-start.1 = (f32[5,3840,128]{2,1,0:T(8,128)S(1)}, f32[5,3840,128]{2,1,0:T(8,128)}, u32[]{:S(2)}) copy-start(f32[5,3840,128]{2,1,0:T(8,128)} %shard_map.56.refs_5_) | copy-start | bytes 29491204
